TPU v7x, 256 devices: a whole 4x4x8 slice. The times are simulated.
256 devices in a mesh: freq: 2 (over y_lo), row: 32 (over x, z), col: 4 (over y_hi, core).
Axes of the slice: x: 4, y: 4 (y_hi: 2, y_lo: 2; y = y_hi * 2 + y_lo), z: 8, core: 2. Of those that a mesh axis runs over, the one named last changes fastest.
Arguments:
- reflection: bfloat16 [8, 2, 8192, 8192], P('freq', None, 'row', 'col'), may hold values from -0.046875 to 0.046875
- panels: bfloat16 [8, 2, 2, 16, 8192], P('freq', None, None, None, ('col', 'row')), may hold values from -6 to 6
- onsets: int32 [16, 8192], P(None, 'row'), may hold values from 128 to 1024
Outputs:
- updates: float32 [32, 1024, 8192], P('col', 'freq', 'row')
All inputs are finite; a program needn't handle non-finite values.
Results may differ from a plain program's by a relative error of at most 0.0003.
Values may be sent and summed in bfloat16 or wider, within the bound.
A program may use at most 64 MiB of HBM per device.

v0:
```python
import jax
import jax.numpy as jnp
from jax import lax
from jax.sharding import PartitionSpec as P

NT = 1024


decay = 2.0
bin_step = 37


def to_times(spectra, first_time, time_count, total_time):
    freq_count = spectra.shape[0]
    times = first_time + jnp.arange(time_count, dtype=jnp.int32)
    bins = bin_step * (jnp.arange(freq_count, dtype=jnp.int32) + 1)
    phase_int = bins[:, None] * times[None, :] % total_time
    phase = phase_int.astype(jnp.float32) * jnp.float32(2.0 * 3.141592653589793 / total_time)
    series = jnp.einsum(
        "kcr,kt->ctr", spectra[:, 0], jnp.cos(phase), precision=lax.Precision.HIGHEST
    )
    return series - jnp.einsum(
        "kcr,kt->ctr", spectra[:, 1], jnp.sin(phase), precision=lax.Precision.HIGHEST
    )


def shards(reflection, panels, onsets):
    freq_here = reflection.shape[0]
    focal = panels.shape[3]
    groups = lax.axis_size("freq")
    freq_total = freq_here * groups
    total_time = NT
    time_here = total_time // groups
    segment = lax.all_gather(panels, "row", axis=4, tiled=True)
    width = segment.shape[4]
    real_rows = segment[:, 0].reshape(freq_here, 2 * focal, width)
    imag_rows = segment[:, 1].reshape(freq_here, 2 * focal, width)
    first = jnp.einsum(
        "fcs,frs->fcr", real_rows, reflection[:, 0], preferred_element_type=jnp.float32
    )
    second = jnp.einsum(
        "fcs,frs->fcr", imag_rows, reflection[:, 1], preferred_element_type=jnp.float32
    )
    third = jnp.einsum(
        "fcs,frs->fcr", imag_rows, reflection[:, 0], preferred_element_type=jnp.float32
    )
    fourth = jnp.einsum(
        "fcs,frs->fcr", real_rows, reflection[:, 1], preferred_element_type=jnp.float32
    )
    parts = jnp.stack([first, second, third, fourth], axis=1)
    signs = jnp.concatenate([jnp.ones((focal,), jnp.float32), -jnp.ones((focal,), jnp.float32)])[
        None, :, None
    ]
    spectra = jnp.stack(
        [parts[:, 0] - signs * parts[:, 1], parts[:, 2] + signs * parts[:, 3]], axis=1
    )
    group_index = lax.axis_index("freq")
    every_freq = lax.all_gather(spectra, "freq", axis=0, tiled=True)
    summed = lax.psum_scatter(every_freq, "col", scatter_dimension=2, tiled=True)
    series = to_times(summed, group_index * time_here, time_here, total_time)
    rows_here = series.shape[0]
    times = group_index * time_here + jnp.arange(time_here, dtype=jnp.int32)
    weight = jnp.exp(-decay * times.astype(jnp.float32) / total_time) / jnp.sqrt(
        jnp.float32(freq_total)
    )
    stacked = jnp.concatenate([onsets, onsets], axis=0)
    mine = lax.dynamic_slice_in_dim(stacked, lax.axis_index("col") * rows_here, rows_here, 0)
    keep = times[None, :, None] < mine[:, None, :]
    return jnp.where(keep, series * weight[None, :, None], jnp.float32(0.0))


def solution(mesh):
    return jax.shard_map(
        shards,
        mesh=mesh,
        in_specs=(
            P("freq", None, "row", "col"),
            P("freq", None, None, None, ("col", "row")),
            P(None, "row"),
        ),
        out_specs=P("col", "freq", "row"),
        check_vma=False,
    )
```

profile of v0, /device:TPU:1, one launch (start us, length us, event | category | flops | bytes accessed | tf_op | source)
XLA Modules:
  0.0 200.1 jit_solution(18324626004792523397)
XLA Ops:
  6.5 0.0 all-gather.2.cloned.1.call-start
  6.5 1.8 copy.8
  8.3 0.0 all-gather.2.cloned.1.call-update
  8.3 0.0 reduce-scatter.2.cloned.1.call-start
  8.4 103.3 %all-gather.2.cloned.1.call-done = bf16[4,2,2,16,2048]{3,0,2,1,4:T(4,128)(2,1)} async-done(((bf16[4,2,2,16,64]{3,0,2,1,4:T(4,128)(2,1)}), bf16[4,2,2,16,2048]{3,0,2,1,4:T(4,128)(2,1)}) %all-gather.2.cloned.1.call-update) | async-done | bytes 1048592 | tf_op jit(solution)/shard_map/all_gather | solution.py:34
  111.6 8.1 %fusion.51 = (bf16[4,1,2,16,2048]{3,0,2,1,4:T(4,128)(2,1)}, bf16[4,1,2,16,2048]{3,0,2,1,4:T(4,128)(2,1)}) fusion(bf16[4,2,2,16,2048]{3,0,2,1,4:T(4,128)(2,1)} %all-gather.2.cloned.1.call-done), kind=kLoop, calls=%fused_computation.51 | loop fusion | bytes 2097152 | tf_op jit(solution)/shard_map/slice | solution.py:37
  119.8 0.0 copy-start.1
  119.8 5.5 %copy.11 = bf16[4,1,2,16,2048]{4,3,2,0,1:T(8,128)(2,1)S(1)} copy(bf16[4,1,2,16,2048]{3,0,2,1,4:T(4,128)(2,1)} %get-tuple-element.5) | data formatting | bytes 1048576 | tf_op jit(solution)/shard_map/slice | solution.py:37
  125.3 5.5 %copy.9 = bf16[4,1,2,16,2048]{4,3,2,0,1:T(8,128)(2,1)S(1)} copy(bf16[4,1,2,16,2048]{3,0,2,1,4:T(4,128)(2,1)} %get-tuple-element.6) | data formatting | bytes 1048576 | tf_op jit(solution)/shard_map/slice | solution.py:36
  130.8 0.0 copy-done.1
  130.8 0.0 slice-start
  130.8 3.7 %fusion.24 = f32[4,32,256]{2,1,0:T(8,128)S(1)} fusion(bf16[4,32,2048]{2,1,0:T(8,128)(2,1)S(1)} %bitcast.48, bf16[4,2,256,2048]{3,2,1,0:T(8,128)(2,1)} %param.3, f32[32]{0:T(128)S(1)} %copy-done.1), kind=kOutput, calls=%fused_computation.17 | convolution fusion | flops 134250496 | bytes 4849792 | tf_op jit(solution)/shard_map/fcs,frs->fcr/dot_general | solution.py:41
  134.5 0.0 slice-start.1
  134.5 3.7 %fusion.27 = f32[4,32,256]{2,1,0:T(8,128)S(1)} fusion(bf16[4,32,2048]{2,1,0:T(8,128)(2,1)S(1)} %bitcast.50, bf16[4,2,256,2048]{3,2,1,0:T(8,128)(2,1)} %param.3, f32[32]{0:T(128)S(1)} %copy-done.1), kind=kOutput, calls=%fused_computation.18 | convolution fusion | flops 134250496 | bytes 4849792 | tf_op jit(solution)/shard_map/fcs,frs->fcr/dot_general | solution.py:47
  138.2 3.5 %fusion.15 = f32[4,1,32,256]{3,2,0,1:T(8,128)S(1)} fusion(f32[4,32,256]{2,1,0:T(8,128)S(1)} %fusion.24, bf16[4,32,2048]{2,1,0:T(8,128)(2,1)S(1)} %bitcast.51, bf16[4,2,256,2048]{3,2,1,0:T(8,128)(2,1)} %param.3), kind=kOutput, calls=%fused_computation.14 | convolution fusion | flops 134250496 | bytes 4980736 | tf_op jit(solution)/shard_map/fcs,frs->fcr/dot_general | solution.py:38
  141.8 0.0 slice-done
  141.8 0.0 slice-done.1
  141.8 0.0 copy-start
  141.8 1.3 fusion.21
  143.2 7.5 %all_gather.7 = f32[8,2,32,256]{3,2,0,1:T(8,128)} all-gather(f32[4,2,32,256]{3,2,0,1:T(8,128)S(1)} %pad_maximum_fusion), channel_id=1, replica_groups=mesh['freq'=2,'row'=32,'col'=4] {'freq'}, dimensions={0}, use_global_device_ids=true | all-gather | bytes 786432 | tf_op jit(solution)/shard_map/all_gather | solution.py:58
  150.7 0.0 reduce-scatter.2.cloned.1.call-update
  150.8 0.0 copy-done
  150.8 32.3 %reduce-scatter.2.cloned.1.call-done = f32[8,2,8,256]{3,2,0,1:T(8,128)} async-done(((f32[8,2,32,256]{3,2,0,1:T(8,128)}), f32[8,2,8,256]{3,2,0,1:T(8,128)}) %reduce-scatter.2.cloned.1.call-update) | async-done | bytes 131088 | tf_op jit(solution)/shard_map/reduce_scatter | solution.py:59
  183.0 0.9 slice_bitcast_fusion
  183.9 3.6 %fusion.31 = f32[512,8,256]{2,0,1:T(8,128)S(1)} fusion(f32[8,8,256]{2,1,0:T(8,128)S(1)} %get-tuple-element.8, s32[512]{0:T(512)S(1)} %iota_add_fusion, s32[8]{0:T(128)S(1)} %add_multiply_fusion), kind=kOutput, calls=%fused_computation.23 | convolution fusion | flops 100720640 | bytes 4261920 | tf_op jit(solution)/shard_map/kcr,kt->ctr/dot_general | solution.py:19
  187.6 5.7 %bitcast_select_fusion = f32[8,512,256]{2,1,0:T(8,128)} fusion(f32[512,8,256]{2,0,1:T(8,128)S(1)} %fusion.31, f32[512]{0:T(512)S(1)} %exponential_multiply_fusion, s32[8,256]{1,0:T(8,128)S(1)} %fusion.40, s32[512]{0:T(512)S(1)} %iota_add_fusion, f32[8,8,256]{2,1,0:T(8,128)S(1)} %get-tuple-element.7, s32[8]{0:T(128)S(1)} %add_multiply_fusion), kind=kOutput, calls=%fused_computation.8 | convolution fusion | flops 104914944 | bytes 8466464 | tf_op jit(solution)/shard_map/kcr,kt->ctr/dot_general | solution.py:22
  (6 shorter events, 0.1 us)
Async XLA Ops:
  6.5 105.1 %all-gather.2.cloned.1.call-start = ((), (), s32[]{:S(2)}) async-start(), calls=%async_computation.1 | async-start | bytes 8650752 | tf_op jit(solution)/shard_map/all_gather | solution.py:34
  8.3 174.7 %reduce-scatter.2.cloned.1.call-start = ((), (), s32[]{:S(2)}) async-start(), calls=%async_computation.2 | async-start | bytes 655360 | tf_op jit(solution)/shard_map/reduce_scatter | solution.py:59
  119.8 11.0 %copy-start.1 = (f32[32]{0:T(128)S(1)}, f32[32]{0:T(128)}, u32[]{:S(2)}) copy-start(f32[32]{0:T(128)} %constant.47.clone.1) | copy-start | bytes 388
  130.8 11.0 %slice-start = ((s8[8388608]{0:T(1024)(128)(4,1)}), s8[4194304]{0:T(1024)(128)(4,1)S(1)}, s32[]{:S(2)}) async-start(s8[8388608]{0:T(1024)(128)(4,1)} %bitcast.52), calls=%async_computation.3 | async-start | bytes 8388608
  134.5 7.3 %slice-start.1 = ((s8[8388608]{0:T(1024)(128)(4,1)}), s8[4194304]{0:T(1024)(128)(4,1)S(1)}, s32[]{:S(2)}) async-start(s8[8388608]{0:T(1024)(128)(4,1)} %bitcast.52), calls=%async_computation.4 | async-start | bytes 8388608
  141.8 9.0 %copy-start = (s32[16,256]{1,0:T(8,128)S(1)}, s32[16,256]{1,0:T(8,128)}, u32[]{:S(2)}) copy-start(s32[16,256]{1,0:T(8,128)} %param.5) | copy-start | bytes 49156
Sparse Core Ops, SparseCore 0:
  9.9 101.6 all-gather.1
  150.8 32.1 reduce-scatter.1
where the time goes:
time: 201 us; the launch traced here: 200 us
  waiting for transfers between devices  136 us (68%)
  local copies, waits for them, and re-layouts  21.8 us (11%)
  matrix products  21.6 us (11%)
  between operations  13.6 us (7%)
  blocking collectives  7.5 us (4%)
    all_gather x1, waiting for transfers between devices, shards(): segment = lax.all_gather(panels, 'row', axis=4, tiled=True)  103 us
    reduce_scatter x1, waiting for transfers between devices, shards(): lax.psum_scatter(every_freq, 'col', scatter_dimension=2, tiled=True)  32.3 us
    slice x2, local copies, waits for them, and re-layouts, shards(): imag_rows = segment[:, 1].reshape(freq_here, 2 * focal, width)  13.6 us
    all_gather x1, blocking collectives, shards(): every_freq = lax.all_gather(spectra, 'freq', axis=0, tiled=True)  7.5 us
    dot_general x1, matrix products, to_times(): jnp.einsum('kcr,kt->ctr', spectra[:, 1], jnp.sin(phase), precision=lax.Pr...  5.74 us
    slice x1, local copies, waits for them, and re-layouts, shards(): real_rows = segment[:, 0].reshape(freq_here, 2 * focal, width)  5.49 us
  transfers between devices with their start and end apart: 2, of which 2 were waited for; matrix products, arithmetic and copies ran while one was open for 0% of the time, Pallas kernels for 0%

commit v1 on v0

v1 whole, which is shorter than its diff:
```python
import functools

import jax
import jax.numpy as jnp
import ml_dtypes
import numpy as np
from jax import lax
from jax.experimental import pallas as pl
from jax.experimental.pallas import tpu as pltpu
from jax.sharding import PartitionSpec as P

NT = 1024
decay = 2.0
bin_step = 37

MESH = pl.DeviceIdType.MESH
BF16 = jnp.bfloat16
F32 = jnp.float32

NX, NZ = 4, 8
FREQS = 4
CHUNKS = 2
PER = FREQS // CHUNKS
NFOC = 16
OWN = 3

GROUPS = ((3, 1), (1, 2), (4, 2), (0, 1), (6, 2))
XSTEPS = (1, 3, 2)


def gather_kernel(
    refl, panels, out, rbuf, praw, held, pmat, sendbuf, slots, load_sem, z_send, z_recv, x_send, x_recv, e_send, e_recv
):
    freq = lax.axis_index("freq")
    row = lax.axis_index("row")
    col = lax.axis_index("col")
    x, z = row // NZ, row % NZ

    def along_z(d):
        return {"row": x * NZ + (z + d + NZ) % NZ}

    def along_x(d):
        return {"row": ((x + d) % NX) * NZ + z}

    def peer(a, b):
        c = (col // 2 + b // 2) % 2 * 2 + (col + b) % 2
        return {"freq": (freq + a) % 2, "col": c}

    peers = [(a, b) for a in range(2) for b in range(4) if (a, b) != (0, 0)]

    barrier = pltpu.get_barrier_semaphore()
    near = [along_z(d) for d in (1, -1, 2, -2)] + [along_x(d) for d in XSTEPS]
    near += [peer(a, b) for a, b in peers]
    for device in near:
        pl.semaphore_signal(barrier, inc=1, device_id=device, device_id_type=MESH)

    load_panels = pltpu.make_async_copy(panels, praw, load_sem.at[FREQS])
    load_panels.start()
    loads = [pltpu.make_async_copy(refl.at[f], rbuf.at[f], load_sem.at[f]) for f in range(FREQS)]
    for load in loads:
        load.start()
    load_panels.wait()

    odd = (z % 2) == 1
    for f in range(FREQS):
        for d in range(2):
            re = praw[f, 0, d].astype(F32)
            im = praw[f, 1, d].astype(F32)
            left = jnp.where(odd, im, re)
            right = jnp.where(odd, re, im)
            held[f // PER, 0, OWN, d, f % PER] = jnp.concatenate([left, right], axis=1).astype(BF16)

    pl.semaphore_wait(barrier, len(near))

    started = []

    def z_copy(c, i, src, dst, step):
        return pltpu.make_async_remote_copy(
            src_ref=held.at[(c, 0) + src],
            dst_ref=held.at[(c, 0) + dst],
            send_sem=z_send.at[c, i],
            recv_sem=z_recv.at[c, i],
            device_id=along_z(step),
            device_id_type=MESH,
        )

    first = ((1, 0), (-1, 1), (2, 2), (-2, 3))

    def z_first(c, step, i):
        return z_copy(c, i, (OWN,), (OWN - step,), step)

    def z_second(c):
        return [
            z_copy(c, 4, (OWN - 2,), (OWN - 3,), 1),
            z_copy(c, 5, (OWN + 2,), (OWN + 3,), -1),
            z_copy(c, 6, (OWN - 2, 0), (OWN + 4, 0), 2),
            z_copy(c, 7, (OWN + 2, 1), (OWN + 4, 1), -2),
        ]

    def x_copies(c, g):
        at, count = GROUPS[g]
        return [
            pltpu.make_async_remote_copy(
                src_ref=held.at[c, 0, pl.ds(at, count)],
                dst_ref=held.at[c, (NX - step) % NX, pl.ds(at, count)],
                send_sem=x_send.at[c, g, i],
                recv_sem=x_recv.at[c, g, i],
                device_id=along_x(step),
                device_id_type=MESH,
            )
            for i, step in enumerate(XSTEPS)
        ]

    def start(copies):
        for copy in copies:
            copy.start()
            started.append(copy)

    for c in range(CHUNKS):
        start([z_first(c, step, i) for step, i in first])
        start(x_copies(c, 0))
    for c in range(CHUNKS):
        for step, i in first:
            z_first(c, step, i).wait_recv()
        start(z_second(c))
        start(x_copies(c, 1))
        start(x_copies(c, 2))
    for c in range(CHUNKS):
        for copy in z_second(c):
            copy.wait_recv()
        start(x_copies(c, 3))
        start(x_copies(c, 4))

    def e_copy(f, a, b):
        c = (col // 2 + b // 2) % 2 * 2 + (col + b) % 2
        return pltpu.make_async_remote_copy(
            src_ref=sendbuf.at[f, c],
            dst_ref=slots.at[a, f, b],
            send_sem=e_send.at[f, a, b],
            recv_sem=e_recv.at[f, a, b],
            device_id=peer(a, b),
            device_id_type=MESH,
        )

    over_sources = (((1,), (1,)), ((), ()))
    lower = lax.broadcasted_iota(jnp.int32, (NFOC, 128), 1) < 64
    for c in range(CHUNKS):
        for g in range(len(GROUPS)):
            for copy in x_copies(c, g):
                copy.wait_recv()
        for i in range(PER):
            f = c * PER + i
            for d in range(2):
                for xa in range(NX):
                    xs = (xa - x + NX) % NX
                    for zp in range(NZ // 2):
                        even = held[c, xs, (2 * zp - z + OWN + NZ) % NZ, d, i].astype(F32)
                        uneven = held[c, xs, (2 * zp + 1 - z + OWN + NZ) % NZ, d, i].astype(F32)
                        at = (xa * NZ // 2 + zp) * 128
                        re = jnp.where(lower, even, uneven)
                        im = pltpu.roll(jnp.where(lower, uneven, even), 64, 1)
                        pmat[pl.ds(d * 16, 16), pl.ds(at, 128)] = re.astype(BF16)
                        pmat[pl.ds(32 + d * 16, 16), pl.ds(at, 128)] = im.astype(BF16)
            loads[f].wait()
            with_re = lax.dot_general(pmat[...], rbuf[f, 0], over_sources, preferred_element_type=F32)
            with_im = lax.dot_general(pmat[...], rbuf[f, 1], over_sources, preferred_element_type=F32)
            for q in range(4):
                here = slice(8 * q, 8 * q + 8)
                there = slice(32 + 8 * q, 40 + 8 * q)
                if q < 2:
                    sendbuf[f, q, 0] = with_re[here] - with_im[there]
                    sendbuf[f, q, 1] = with_re[there] + with_im[here]
                else:
                    sendbuf[f, q, 0] = with_re[here] + with_im[there]
                    sendbuf[f, q, 1] = with_re[there] - with_im[here]
            start([e_copy(f, a, b) for a, b in peers])

    def keep(k, part, value):
        for h in range(out.shape[0]):
            out[h, pl.ds((k * 2 + part) * 8, 8), :] = value[:, 128 * h : 128 * h + 128]

    for f in range(FREQS):
        for a, b in peers:
            e_copy(f, a, b).wait_recv()
        for part in range(2):
            near_sum = sendbuf[f, col, part] + slots[0, f, 1, part]
            near_sum += slots[0, f, 2, part] + slots[0, f, 3, part]
            keep(f, part, near_sum)
            far_sum = slots[1, f, 0, part] + slots[1, f, 1, part]
            far_sum += slots[1, f, 2, part] + slots[1, f, 3, part]
            keep(f + FREQS, part, far_sum)
    for copy in started:
        copy.wait_send()


def times_kernel(spectra, table, onsets, out, series, out_sem):
    freq = lax.axis_index("freq")
    col = lax.axis_index("col")
    steps = series.shape[1]
    width = series.shape[2]
    basis = table[freq]
    times = freq * steps + lax.broadcasted_iota(jnp.int32, (steps, width), 0)
    limits = onsets[pl.ds(pl.multiple_of(col % 2 * 8, 8), 8), :]
    copies = []
    for c in range(8):
        values = jnp.concatenate(
            [spectra[h, pl.ds(c, 16, stride=8), :] for h in range(width // 128)], axis=1
        )
        high = values.astype(BF16)
        low = (values - high.astype(F32)).astype(BF16)
        parts = jnp.concatenate([high, high, low, low], axis=0)
        found = jnp.dot(basis, parts, preferred_element_type=F32)
        series[c] = jnp.where(times < limits[c : c + 1, :], found, 0.0)
        copy = pltpu.make_async_copy(series.at[c], out.at[c], out_sem.at[c])
        copy.start()
        copies.append(copy)
    for copy in copies:
        copy.wait()


def make_table(groups, freq_here):
    total = groups * freq_here
    t = np.arange(NT, dtype=np.int64)
    weight = np.exp(-decay * t / NT) / np.sqrt(total)
    halves = []
    for g in range(groups):
        mine = slice(g * NT // groups, (g + 1) * NT // groups)
        columns = []
        for a in range(groups):
            for f in range(freq_here):
                k = (g + a) % groups * freq_here + f
                phase = 2.0 * np.pi * ((bin_step * (k + 1) * t) % NT) / NT
                columns += [(np.cos(phase) * weight)[mine], (-np.sin(phase) * weight)[mine]]
        whole = np.stack(columns, axis=1)
        high = whole.astype(np.float32).astype(ml_dtypes.bfloat16)
        low = (whole - high.astype(np.float64)).astype(np.float32).astype(ml_dtypes.bfloat16)
        halves.append(np.concatenate([high, low, high, low], axis=1))
    return np.stack(halves)


def shards(reflection, panels, onsets):
    receivers = reflection.shape[2]
    sources = reflection.shape[3]
    vmem = pl.BlockSpec(memory_space=pltpu.VMEM)
    hbm = pl.BlockSpec(memory_space=pl.ANY)
    spectra = pl.pallas_call(
        gather_kernel,
        out_shape=jax.ShapeDtypeStruct((receivers // 128, 128, 128), F32),
        in_specs=[hbm, hbm],
        out_specs=vmem,
        scratch_shapes=[
            pltpu.VMEM(reflection.shape, BF16),
            pltpu.VMEM(panels.shape, BF16),
            pltpu.VMEM((CHUNKS, NX, NZ, 2, PER, NFOC, 128), BF16),
            pltpu.VMEM((64, sources), BF16),
            pltpu.VMEM((FREQS, 4, 2, 8, receivers), F32),
            pltpu.VMEM((2, FREQS, 4, 2, 8, receivers), F32),
            pltpu.SemaphoreType.DMA((FREQS + 1,)),
            pltpu.SemaphoreType.DMA((CHUNKS, 8)),
            pltpu.SemaphoreType.DMA((CHUNKS, 8)),
            pltpu.SemaphoreType.DMA((CHUNKS, len(GROUPS), 3)),
            pltpu.SemaphoreType.DMA((CHUNKS, len(GROUPS), 3)),
            pltpu.SemaphoreType.DMA((FREQS, 2, 4)),
            pltpu.SemaphoreType.DMA((FREQS, 2, 4)),
        ],
        compiler_params=pltpu.CompilerParams(collective_id=0, has_side_effects=True, vmem_limit_bytes=48 << 20),
        name="gather_products",
    )(reflection, panels)
    groups = lax.axis_size("freq")
    steps = NT // groups
    table = jnp.asarray(make_table(groups, reflection.shape[0]))
    return pl.pallas_call(
        times_kernel,
        out_shape=jax.ShapeDtypeStruct((8, steps, receivers), F32),
        in_specs=[vmem, vmem, vmem],
        out_specs=hbm,
        scratch_shapes=[pltpu.VMEM((8, steps, receivers), F32), pltpu.SemaphoreType.DMA((8,))],
        compiler_params=pltpu.CompilerParams(vmem_limit_bytes=48 << 20),
        name="to_times",
    )(spectra, table, onsets)


def solution(mesh):
    return jax.shard_map(
        shards,
        mesh=mesh,
        in_specs=(
            P("freq", None, "row", "col"),
            P("freq", None, None, None, ("col", "row")),
            P(None, "row"),
        ),
        out_specs=P("col", "freq", "row"),
        check_vma=False,
    )
```

time: 201 us -> 38 us (0.19)
  waiting for transfers between devices: 136 us -> 0 us
  Pallas kernels: 0 us -> 37 us
  matrix products: 21.6 us -> 0 us
  local copies, waits for them, and re-layouts: 21.8 us -> 0.89 us
  between operations: 13.6 us -> 0.03 us
  blocking collectives: 7.5 us -> 0 us
    all_gather x1 -> x0, waiting for transfers between devices: 103 us -> none  [shards(): segment = lax.all_gather(panels, 'row', axis=4, tiled=True)]
    pallas_call x0 -> x2, Pallas kernels: none -> 37 us  [the longest x1 34.7 us: shards(): pl.pallas_call(gather_kernel, out_shape=jax.ShapeDtypeStruct((receivers /...]
    reduce_scatter x1 -> x0, waiting for transfers between devices: 32.3 us -> none  [shards(): lax.psum_scatter(every_freq, 'col', scatter_dimension=2, tiled=True)]
    dot_general x6 -> x0, matrix products: 21.6 us -> none  [the longest x1 5.74 us: to_times(): jnp.einsum('kcr,kt->ctr', spectra[:, 1], jnp.sin(phase), precision=lax.Pr...]
    slice x3 -> x0, local copies, waits for them, and re-layouts: 19.1 us -> none  [the longest x2 13.6 us: shards(): imag_rows = segment[:, 1].reshape(freq_here, 2 * focal, width)]
    all_gather x1 -> x0, blocking collectives: 7.5 us -> none  [shards(): every_freq = lax.all_gather(spectra, 'freq', axis=0, tiled=True)]
  transfers between devices with their start and end apart: 2 -> 0, of which waited for: 2 -> 0; matrix products, arithmetic and copies ran while one was open for 0% -> 0% of each run, Pallas kernels for 0% -> 0%
where the time goes in v1:
time: 38 us; the launch traced here: 37.9 us
  Pallas kernels  37 us (97%)
  local copies, waits for them, and re-layouts  0.89 us (2%)
    pallas_call x1, Pallas kernels, shards(): pl.pallas_call(gather_kernel, out_shape=jax.ShapeDtypeStruct((receivers /...  34.7 us
    pallas_call x1, Pallas kernels, shards(): pl.pallas_call(times_kernel, out_shape=jax.ShapeDtypeStruct((8, steps, re...  2.35 us
    unnamed x6, local copies, waits for them, and re-layouts  0.89 us

profile of v1, /device:TPU:1, one launch (start us, length us, event | category | flops | bytes accessed | tf_op | source)
XLA Modules:
  0.0 37.9 jit_solution(7561047238825431466)
XLA Ops:
  0.0 0.0 copy-start
  0.0 0.0 copy-start.1
  0.0 0.9 %copy-done.1 = bf16[4,2,2,16,64]{4,3,2,1,0:T(8,128)(2,1)S(1)} copy-done((bf16[4,2,2,16,64]{4,3,2,1,0:T(8,128)(2,1)S(1)}, bf16[4,2,2,16,64]{4,3,2,1,0:T(8,128)(2,1)}, u32[]{:S(2)}) %copy-start.1) | copy-done | bytes 32792
  0.9 0.0 copy-start.2
  0.9 34.7 %gather_products.1.spectra = f32[2,128,128]{2,1,0:T(8,128)S(1)} custom-call(bf16[4,2,256,2048]{3,2,1,0:T(8,128)(2,1)} %refl.1, bf16[4,2,2,16,64]{4,3,2,1,0:T(8,128)(2,1)S(1)} %copy-done.1), custom_call_target="tpu_custom_call" | custom-call | tf_op jit(solution)/shard_map/gather_products/pallas_call | solution.py:246
  35.6 0.0 copy-done
  35.6 0.0 copy-done.2
  35.6 2.3 %to_times.1 = f32[8,512,256]{2,1,0:T(8,128)} custom-call(f32[2,128,128]{2,1,0:T(8,128)S(1)} %gather_products.1.spectra, bf16[2,512,64]{2,1,0:T(8,128)(2,1)S(1)} %copy-done, s32[16,256]{1,0:T(8,128)S(1)} %copy-done.2), custom_call_target="tpu_custom_call" | custom-call | tf_op jit(solution)/shard_map/to_times/pallas_call | solution.py:272
Async XLA Ops:
  0.0 35.6 %copy-start = (bf16[2,512,64]{2,1,0:T(8,128)(2,1)S(1)}, bf16[2,512,64]{2,1,0:T(8,128)(2,1)}, u32[]{:S(2)}) copy-start(bf16[2,512,64]{2,1,0:T(8,128)(2,1)} %constant.2.clone.table) | copy-start | bytes 393220
  0.0 0.9 %copy-start.1 = (bf16[4,2,2,16,64]{4,3,2,1,0:T(8,128)(2,1)S(1)}, bf16[4,2,2,16,64]{4,3,2,1,0:T(8,128)(2,1)}, u32[]{:S(2)}) copy-start(bf16[4,2,2,16,64]{4,3,2,1,0:T(8,128)(2,1)} %panels.1) | copy-start | bytes 98308
  0.9 34.7 %copy-start.2 = (s32[16,256]{1,0:T(8,128)S(1)}, s32[16,256]{1,0:T(8,128)}, u32[]{:S(2)}) copy-start(s32[16,256]{1,0:T(8,128)} %onsets.1) | copy-start | bytes 49156

commit v2 on v1

v2 whole, which is shorter than its diff:
```python
import functools

import jax
import jax.numpy as jnp
import ml_dtypes
import numpy as np
from jax import lax
from jax.experimental import pallas as pl
from jax.experimental.pallas import tpu as pltpu
from jax.sharding import PartitionSpec as P

NT = 1024
decay = 2.0
bin_step = 37

MESH = pl.DeviceIdType.MESH
BF16 = jnp.bfloat16
F32 = jnp.float32

NX, NZ = 4, 8
FREQS = 4
NFOC = 16
OWN = 3
PART = NZ * 64

Z_FIRST, X_FIRST = 0, 1
TILES = (5, 3)


def tile(f, d):
    if d == 0:
        return Z_FIRST, f
    return (Z_FIRST, 4) if f == 0 else (X_FIRST, f - 1)

def gather_kernel(
    refl, panels, out, rbuf, praw, held_z, held_x, pmat, acc, sendbuf, slots,
    load_sem, h_send, h_recv, e_send, e_recv,
):
    held = (held_z, held_x)
    freq = lax.axis_index("freq")
    row = lax.axis_index("row")
    col = lax.axis_index("col")
    x, z = row // NZ, row % NZ
    core, far = col % 2, col // 2

    along = {("z", d): {"row": x * NZ + (z + d + NZ) % NZ} for d in (1, -1, 2, -2)}
    along |= {("x", d): {"row": ((x + d + NX) % NX) * NZ + z} for d in (1, -1, 2)}

    def column(b):
        return (far + b // 2) % 2 * 2 + (core + b) % 2

    def peer(a, b):
        return {"freq": (freq + a) % 2, "col": column(b)}

    peers = ((0, 2), (0, 3), (1, 2), (1, 3), (1, 0), (1, 1), (0, 1))

    barrier = pltpu.get_barrier_semaphore()
    near = list(along.values()) + [peer(a, b) for a, b in peers]
    for device in near:
        pl.semaphore_signal(barrier, inc=1, device_id=device, device_id_type=MESH)

    load_panels = pltpu.make_async_copy(panels, praw, load_sem.at[FREQS])
    load_panels.start()
    loads = [pltpu.make_async_copy(refl.at[f], rbuf.at[f], load_sem.at[f]) for f in range(FREQS)]
    for load in loads:
        load.start()
    load_panels.wait()

    odd = (z % 2) == 1
    for f in range(FREQS):
        for d in range(2):
            re = praw[f, 0, d].astype(F32)
            im = praw[f, 1, d].astype(F32)
            left = jnp.where(odd, im, re)
            right = jnp.where(odd, re, im)
            kind, i = tile(f, d)
            held[kind][0, OWN, i] = jnp.concatenate([left, right], axis=1).astype(BF16)

    pl.semaphore_wait(barrier, len(near))

    started = []

    def start(copies):
        for copy in copies:
            copy.start()
            started.append(copy)

    def arrived(copies):
        for copy in copies:
            copy.wait_recv()

    def slot(dx, dz):
        return dx % NX, (4 if dz == -4 else dz) + OWN

    def hop(kind, dx, dz, axis, step, count=1):
        there = slot(dx + step, dz) if axis == "x" else slot(dx, dz + step)
        (x_from, z_from), (x_to, z_to) = slot(dx, dz), there
        return pltpu.make_async_remote_copy(
            src_ref=held[kind].at[x_from, pl.ds(z_from, count)],
            dst_ref=held[kind].at[x_to, pl.ds(z_to, count)],
            send_sem=h_send.at[kind, x_to, z_to],
            recv_sem=h_recv.at[kind, x_to, z_to],
            device_id=along[axis, step],
            device_id_type=MESH,
        )

    def here(kind, dx, dz, count=1):
        x_at, z_at = slot(dx, dz)
        at = held[kind].at[x_at, pl.ds(z_at, count)]
        return pltpu.make_async_remote_copy(
            src_ref=at,
            dst_ref=at,
            send_sem=h_send.at[kind, x_at, z_at],
            recv_sem=h_recv.at[kind, x_at, z_at],
            device_id=along["x", 1],
            device_id_type=MESH,
        )

    def round_x(kind, dz, count=1):
        return [hop(kind, 0, dz, "x", step, count) for step in (2, 1, -1)]

    def along_z(kind, dx, dz):
        if dz == 0:
            steps = (2, -2, 1, -1)
        else:
            way = dz // 2
            both = way == (1 if kind == Z_FIRST or dx == 0 else -1)
            steps = (2 * way, way) if both else (way,)
        return [hop(kind, dx, dz, "z", step) for step in steps]

    over_sources = (((1,), (1,)), ((), ()))
    lower = lax.broadcasted_iota(jnp.int32, (NFOC, 128), 1) < 64
    z_slots = [(z - za + OWN + NZ) % NZ for za in range(NZ)]

    def multiply(f, ways):
        found = [acc[f, m] if 0 not in ways else None for m in range(2)]
        for i, dx in enumerate(ways):
            for d in range(2):
                kind, t = tile(f, d)
                for zp in range(NZ // 2):
                    even = held[kind][dx % NX, z_slots[2 * zp], t].astype(F32)
                    uneven = held[kind][dx % NX, z_slots[2 * zp + 1], t].astype(F32)
                    re = jnp.where(lower, even, uneven)
                    im = pltpu.roll(jnp.where(lower, uneven, even), 64, 1)
                    at = pl.ds(i * PART + zp * 128, 128)
                    pmat[pl.ds(d * 16, 16), at] = re.astype(BF16)
                    pmat[pl.ds(32 + d * 16, 16), at] = im.astype(BF16)
        for i, dx in enumerate(ways):
            sources = pl.ds(pl.multiple_of((x - dx + NX) % NX * PART, PART), PART)
            for m in range(2):
                more = lax.dot_general(
                    pmat[:, i * PART : i * PART + PART],
                    rbuf[f, m, :, sources],
                    over_sources,
                    preferred_element_type=F32,
                )
                found[m] = more if found[m] is None else found[m] + more
        for m in range(2):
            acc[f, m] = found[m]

    def e_copy(f, a, b):
        return pltpu.make_async_remote_copy(
            src_ref=sendbuf.at[f, column(b)],
            dst_ref=slots.at[f, a, b],
            send_sem=e_send.at[f, a, b],
            recv_sem=e_recv.at[f, a, b],
            device_id=peer(a, b),
            device_id_type=MESH,
        )

    def combine(f):
        for q in range(4):
            here = pl.ds(8 * q, 8)
            there = pl.ds(32 + 8 * q, 8)
            if q < 2:
                sendbuf[f, q, 0] = acc[f, 0, here] - acc[f, 1, there]
                sendbuf[f, q, 1] = acc[f, 0, there] + acc[f, 1, here]
            else:
                sendbuf[f, q, 0] = acc[f, 0, here] + acc[f, 1, there]
                sendbuf[f, q, 1] = acc[f, 0, there] - acc[f, 1, here]
        start([e_copy(f, a, b) for a, b in peers])

    def keep(k, part, value):
        for h in range(out.shape[0]):
            out[h, pl.ds((k * 2 + part) * 8, 8), :] = value[:, 128 * h : 128 * h + 128]

    start(along_z(Z_FIRST, 0, 0))
    start(round_x(X_FIRST, 0))
    start(round_x(Z_FIRST, 0))
    start(along_z(X_FIRST, 0, 0))
    for dx in (1, -1):
        arrived([here(X_FIRST, dx, 0)])
        start(along_z(X_FIRST, dx, 0))
    for dz in (2, -2):
        arrived([here(Z_FIRST, 0, dz)])
        start(along_z(Z_FIRST, 0, dz))
    arrived([here(X_FIRST, 2, 0)])
    start(along_z(X_FIRST, 2, 0))
    for dz in (1, -1):
        arrived([here(Z_FIRST, 0, dz)])
    for dz in (1, -2):
        start(round_x(Z_FIRST, dz, 2))
    for dx in (0, 1, -1):
        for dz in (2, -2):
            arrived([here(X_FIRST, dx, dz)])
            start(along_z(X_FIRST, dx, dz))
    arrived([here(Z_FIRST, 0, dz) for dz in (3, 4)])
    start(round_x(Z_FIRST, 3, 2))
    arrived([here(Z_FIRST, 0, -3)])
    start(round_x(Z_FIRST, -3))
    for dz in (2, -2):
        arrived([here(X_FIRST, 2, dz)])
        start(along_z(X_FIRST, 2, dz))
    gathering, started[:] = list(started), []

    for f in range(FREQS):
        if f == 1:
            arrived([here(X_FIRST, 0, dz) for dz in (1, -1, 3, -3, 4)])
        loads[f].wait()
        multiply(f, (0,))
    for dx in (1, -1, 2):
        arrived([here(Z_FIRST, dx, 0)])
        arrived([here(Z_FIRST, dx, dz, 2) for dz in (1, -2, 3)])
        arrived([here(Z_FIRST, dx, -3)])
    for f in range(FREQS):
        if f == 1:
            for dx in (1, -1, 2):
                arrived([here(X_FIRST, dx, dz) for dz in (1, -1, 3, -3, 4)])
        multiply(f, (1, -1, 2))
        combine(f)
    for copy in gathering:
        copy.wait_send()
    for f in range(FREQS):
        arrived([e_copy(f, a, b) for a, b in peers])
        for part in range(2):
            own = sendbuf[f, col, part] + slots[f, 0, 1, part]
            keep(f, part, own + (slots[f, 0, 2, part] + slots[f, 0, 3, part]))
            other = slots[f, 1, 0, part] + slots[f, 1, 1, part]
            keep(f + FREQS, part, other + (slots[f, 1, 2, part] + slots[f, 1, 3, part]))
    for copy in started:
        copy.wait_send()


def times_kernel(spectra, table, onsets, out, series, out_sem):
    freq = lax.axis_index("freq")
    col = lax.axis_index("col")
    steps = series.shape[1]
    width = series.shape[2]
    basis = table[freq]
    times = freq * steps + lax.broadcasted_iota(jnp.int32, (steps, width), 0)
    limits = onsets[pl.ds(pl.multiple_of(col % 2 * 8, 8), 8), :]
    copies = []
    for c in range(8):
        values = jnp.concatenate(
            [spectra[h, pl.ds(c, 16, stride=8), :] for h in range(width // 128)], axis=1
        )
        high = values.astype(BF16)
        low = (values - high.astype(F32)).astype(BF16)
        parts = jnp.concatenate([high, high, low, low], axis=0)
        found = jnp.dot(basis, parts, preferred_element_type=F32)
        series[c] = jnp.where(times < limits[c : c + 1, :], found, 0.0)
        copy = pltpu.make_async_copy(series.at[c], out.at[c], out_sem.at[c])
        copy.start()
        copies.append(copy)
    for copy in copies:
        copy.wait()


def make_table(groups, freq_here):
    total = groups * freq_here
    t = np.arange(NT, dtype=np.int64)
    weight = np.exp(-decay * t / NT) / np.sqrt(total)
    halves = []
    for g in range(groups):
        mine = slice(g * NT // groups, (g + 1) * NT // groups)
        columns = []
        for a in range(groups):
            for f in range(freq_here):
                k = (g + a) % groups * freq_here + f
                phase = 2.0 * np.pi * ((bin_step * (k + 1) * t) % NT) / NT
                columns += [(np.cos(phase) * weight)[mine], (-np.sin(phase) * weight)[mine]]
        whole = np.stack(columns, axis=1)
        high = whole.astype(np.float32).astype(ml_dtypes.bfloat16)
        low = (whole - high.astype(np.float64)).astype(np.float32).astype(ml_dtypes.bfloat16)
        halves.append(np.concatenate([high, low, high, low], axis=1))
    return np.stack(halves)


def shards(reflection, panels, onsets):
    receivers = reflection.shape[2]
    vmem = pl.BlockSpec(memory_space=pltpu.VMEM)
    hbm = pl.BlockSpec(memory_space=pltpu.HBM)
    panels = pltpu.with_memory_space_constraint(panels, pltpu.HBM)
    spectra = pl.pallas_call(
        gather_kernel,
        out_shape=jax.ShapeDtypeStruct((receivers // 128, 128, 128), F32),
        in_specs=[hbm, hbm],
        out_specs=vmem,
        scratch_shapes=[
            pltpu.VMEM(reflection.shape, BF16),
            pltpu.VMEM(panels.shape, BF16),
            *[pltpu.VMEM((NX, NZ, count, NFOC, 128), BF16) for count in TILES],
            pltpu.VMEM((64, 3 * PART), BF16),
            pltpu.VMEM((FREQS, 2, 64, receivers), F32),
            pltpu.VMEM((FREQS, 4, 2, 8, receivers), F32),
            pltpu.VMEM((FREQS, 2, 4, 2, 8, receivers), F32),
            pltpu.SemaphoreType.DMA((FREQS + 1,)),
            pltpu.SemaphoreType.DMA((2, NX, NZ)),
            pltpu.SemaphoreType.DMA((2, NX, NZ)),
            pltpu.SemaphoreType.DMA((FREQS, 2, 4)),
            pltpu.SemaphoreType.DMA((FREQS, 2, 4)),
        ],
        compiler_params=pltpu.CompilerParams(collective_id=0, has_side_effects=True, vmem_limit_bytes=48 << 20),
        name="gather_products",
    )(reflection, panels)
    groups = lax.axis_size("freq")
    steps = NT // groups
    table = jnp.asarray(make_table(groups, reflection.shape[0]))
    return pl.pallas_call(
        times_kernel,
        out_shape=jax.ShapeDtypeStruct((8, steps, receivers), F32),
        in_specs=[vmem, vmem, vmem],
        out_specs=hbm,
        scratch_shapes=[pltpu.VMEM((8, steps, receivers), F32), pltpu.SemaphoreType.DMA((8,))],
        compiler_params=pltpu.CompilerParams(vmem_limit_bytes=48 << 20),
        name="to_times",
    )(spectra, table, onsets)


def solution(mesh):
    return jax.shard_map(
        shards,
        mesh=mesh,
        in_specs=(
            P("freq", None, "row", "col"),
            P("freq", None, None, None, ("col", "row")),
            P(None, "row"),
        ),
        out_specs=P("col", "freq", "row"),
        check_vma=False,
    )
```

time: 38 us -> 34.3 us (0.903)
  Pallas kernels: 37 us -> 34.2 us
  local copies, waits for them, and re-layouts: 0.89 us -> 0.01 us
    pallas_call x1, Pallas kernels: 34.7 us -> 31.9 us  [shards(): pl.pallas_call(gather_kernel, out_shape=jax.ShapeDtypeStruct((receivers /...]
    unnamed x6 -> x4, local copies, waits for them, and re-layouts: 0.89 us -> 0.01 us
where the time goes in v2:
time: 34.3 us; the launch traced here: 34.2 us
  Pallas kernels  34.2 us (100%)
    pallas_call x1, Pallas kernels, shards(): pl.pallas_call(gather_kernel, out_shape=jax.ShapeDtypeStruct((receivers /...  31.9 us
    pallas_call x1, Pallas kernels, shards(): pl.pallas_call(times_kernel, out_shape=jax.ShapeDtypeStruct((8, steps, re...  2.34 us

profile of v2, /device:TPU:1, one launch (start us, length us, event | category | flops | bytes accessed | tf_op | source)
XLA Modules:
  0.0 34.2 jit_solution(2507221999959333084)
XLA Ops:
  0.0 0.0 copy-start
  0.0 0.0 copy-start.1
  0.0 31.9 %gather_products.1.spectra = f32[2,128,128]{2,1,0:T(8,128)S(1)} custom-call(bf16[4,2,256,2048]{3,2,1,0:T(8,128)(2,1)} %refl.1, bf16[4,2,2,16,64]{4,3,2,1,0:T(8,128)(2,1)} %panels.1), custom_call_target="tpu_custom_call" | custom-call | tf_op jit(solution)/shard_map/gather_products/pallas_call | solution.py:294
  31.9 0.0 copy-done
  31.9 0.0 copy-done.1
  31.9 2.3 %to_times.1 = f32[8,512,256]{2,1,0:T(8,128)} custom-call(f32[2,128,128]{2,1,0:T(8,128)S(1)} %gather_products.1.spectra, bf16[2,512,64]{2,1,0:T(8,128)(2,1)S(1)} %copy-done, s32[16,256]{1,0:T(8,128)S(1)} %copy-done.1), custom_call_target="tpu_custom_call" | custom-call | tf_op jit(solution)/shard_map/to_times/pallas_call | solution.py:319
Async XLA Ops:
  0.0 31.9 %copy-start = (bf16[2,512,64]{2,1,0:T(8,128)(2,1)S(1)}, bf16[2,512,64]{2,1,0:T(8,128)(2,1)}, u32[]{:S(2)}) copy-start(bf16[2,512,64]{2,1,0:T(8,128)(2,1)} %constant.2.clone.table) | copy-start | bytes 393220
  0.0 31.9 %copy-start.1 = (s32[16,256]{1,0:T(8,128)S(1)}, s32[16,256]{1,0:T(8,128)}, u32[]{:S(2)}) copy-start(s32[16,256]{1,0:T(8,128)} %onsets.1) | copy-start | bytes 49156

commit v3 on v2

--- a/solution.py
+++ b/solution.py
@@ -54,16 +54,14 @@
 
     peers = ((0, 2), (0, 3), (1, 2), (1, 3), (1, 0), (1, 1), (0, 1))
 
+    load_panels = pltpu.make_async_copy(panels, praw, load_sem.at[FREQS])
+    load_panels.start()
     barrier = pltpu.get_barrier_semaphore()
     near = list(along.values()) + [peer(a, b) for a, b in peers]
     for device in near:
         pl.semaphore_signal(barrier, inc=1, device_id=device, device_id_type=MESH)
 
-    load_panels = pltpu.make_async_copy(panels, praw, load_sem.at[FREQS])
-    load_panels.start()
     loads = [pltpu.make_async_copy(refl.at[f], rbuf.at[f], load_sem.at[f]) for f in range(FREQS)]
-    for load in loads:
-        load.start()
     load_panels.wait()
 
     odd = (z % 2) == 1
@@ -188,6 +186,8 @@
     start(round_x(X_FIRST, 0))
     start(round_x(Z_FIRST, 0))
     start(along_z(X_FIRST, 0, 0))
+    for load in loads:
+        load.start()
     for dx in (1, -1):
         arrived([here(X_FIRST, dx, 0)])
         start(along_z(X_FIRST, dx, 0))
@@ -204,10 +204,9 @@
         for dz in (2, -2):
             arrived([here(X_FIRST, dx, dz)])
             start(along_z(X_FIRST, dx, dz))
-    arrived([here(Z_FIRST, 0, dz) for dz in (3, 4)])
-    start(round_x(Z_FIRST, 3, 2))
-    arrived([here(Z_FIRST, 0, -3)])
-    start(round_x(Z_FIRST, -3))
+    for dz in (3, -3, 4):
+        arrived([here(Z_FIRST, 0, dz)])
+        start(round_x(Z_FIRST, dz))
     for dz in (2, -2):
         arrived([here(X_FIRST, 2, dz)])
         start(along_z(X_FIRST, 2, dz))
@@ -220,15 +219,15 @@
         multiply(f, (0,))
     for dx in (1, -1, 2):
         arrived([here(Z_FIRST, dx, 0)])
-        arrived([here(Z_FIRST, dx, dz, 2) for dz in (1, -2, 3)])
-        arrived([here(Z_FIRST, dx, -3)])
+        arrived([here(Z_FIRST, dx, dz, 2) for dz in (1, -2)])
+        arrived([here(Z_FIRST, dx, dz) for dz in (3, -3, 4)])
     for f in range(FREQS):
         if f == 1:
             for dx in (1, -1, 2):
                 arrived([here(X_FIRST, dx, dz) for dz in (1, -1, 3, -3, 4)])
         multiply(f, (1, -1, 2))
         combine(f)
-    for copy in gathering:
+    for copy in gathering + started:
         copy.wait_send()
     for f in range(FREQS):
         arrived([e_copy(f, a, b) for a, b in peers])
@@ -237,8 +236,6 @@
             keep(f, part, own + (slots[f, 0, 2, part] + slots[f, 0, 3, part]))
             other = slots[f, 1, 0, part] + slots[f, 1, 1, part]
             keep(f + FREQS, part, other + (slots[f, 1, 2, part] + slots[f, 1, 3, part]))
-    for copy in started:
-        copy.wait_send()
 
 
 def times_kernel(spectra, table, onsets, out, series, out_sem):

time: 34.3 us -> 34.1 us (level)
  no operation moved by 1% of the time
where the time goes in v3:
time: 34.1 us; the launch traced here: 34 us
  Pallas kernels  34 us (100%)
    pallas_call x1, Pallas kernels, shards(): pl.pallas_call(gather_kernel, out_shape=jax.ShapeDtypeStruct((receivers /...  31.7 us
    pallas_call x1, Pallas kernels, shards(): pl.pallas_call(times_kernel, out_shape=jax.ShapeDtypeStruct((8, steps, re...  2.35 us

profile of v3, /device:TPU:1, one launch (start us, length us, event | category | flops | bytes accessed | tf_op | source)
XLA Modules:
  0.0 34.0 jit_solution(13339294828404531542)
XLA Ops:
  0.0 0.0 copy-start
  0.0 0.0 copy-start.1
  0.0 31.7 %gather_products.1.spectra = f32[2,128,128]{2,1,0:T(8,128)S(1)} custom-call(bf16[4,2,256,2048]{3,2,1,0:T(8,128)(2,1)} %refl.1, bf16[4,2,2,16,64]{4,3,2,1,0:T(8,128)(2,1)} %panels.1), custom_call_target="tpu_custom_call" | custom-call | tf_op jit(solution)/shard_map/gather_products/pallas_call | solution.py:291
  31.7 0.0 copy-done
  31.7 0.0 copy-done.1
  31.7 2.3 %to_times.1 = f32[8,512,256]{2,1,0:T(8,128)} custom-call(f32[2,128,128]{2,1,0:T(8,128)S(1)} %gather_products.1.spectra, bf16[2,512,64]{2,1,0:T(8,128)(2,1)S(1)} %copy-done, s32[16,256]{1,0:T(8,128)S(1)} %copy-done.1), custom_call_target="tpu_custom_call" | custom-call | tf_op jit(solution)/shard_map/to_times/pallas_call | solution.py:316
Async XLA Ops:
  0.0 31.7 %copy-start = (bf16[2,512,64]{2,1,0:T(8,128)(2,1)S(1)}, bf16[2,512,64]{2,1,0:T(8,128)(2,1)}, u32[]{:S(2)}) copy-start(bf16[2,512,64]{2,1,0:T(8,128)(2,1)} %constant.2.clone.table) | copy-start | bytes 393220
  0.0 31.7 %copy-start.1 = (s32[16,256]{1,0:T(8,128)S(1)}, s32[16,256]{1,0:T(8,128)}, u32[]{:S(2)}) copy-start(s32[16,256]{1,0:T(8,128)} %onsets.1) | copy-start | bytes 49156
